TPU v7x, 256 devices: a whole 4x4x8 slice. The times are simulated.
256 devices in a mesh: user: 32 (over z, x), tp: 8 (over y, core).
Axes of the slice: x: 4, y: 4, z: 8, core: 2. Of those that a mesh axis runs over, the one named last changes fastest.
Arguments:
- cand_feats: bfloat16 [32768, 1024], P('user', 'tp'), may hold values from -6 to 6
- w_in: bfloat16 [1024, 2048], P(None, 'tp'), may hold values from -0.1875 to 0.1875
- w_out: bfloat16 [1024, 1024], P('tp'), may hold values from -0.1875 to 0.1875
- kv_cache: bfloat16 [2048, 128, 2048], P('user', None, 'tp'), may hold values from -6 to 6
- event_mask: int32 [2048, 128], P('user'), may hold values from 0 to 1, as said below
- block_counts: int32 [256], P('user'), may hold values from 1 to 8, as said below
- user_blocks: int32 [256, 8], P('user'), may hold values from 0 to 63, as said below
- send_slots: int32 [1024, 2], P('user'), may hold values from 0 to 63, as said below
- cand_user: int32 [32768], P('user'), may hold values from 0 to 7
Outputs:
- scored: bfloat16 [32768, 1024], P('user', 'tp')
Inputs may be any that keep to these rules, and one draw needn't show every extreme that they name: `block_counts`: on every index of the user axis some user has 8 blocks, and on one index every user has. For user u of the index r of the user axis and j < block_counts[r * 8 + u], user_blocks[r * 8 + u, j] = o * 2 + c says that block j of u's history is cached on index o, in its local row send_slots[o * 32 + r, c] of kv_cache and event_mask. These valid entries of one index's users are all different, and on one index they take all 64 values. Entries with j >= block_counts[u] are arbitrary. `send_slots`: the 32 rows of one holder o (rows o * 32 to o * 32 + 31) name each of its local rows 0 to 63 exactly once. `event_mask`: in every block of a user's history the first event is real.
All inputs are finite; a program needn't handle non-finite values.
Results may differ from a plain program's by a relative error of at most 0.013.
Values may be sent and summed in bfloat16 or wider, within the bound.
A program may use at most 128 MiB of HBM per device.

v0:
```python
import jax
import jax.numpy as jnp
from jax import lax
from jax.sharding import PartitionSpec as P

DH = 128
EVENTS = 128


norm_eps = 1e-06


def owner_users(block_count, block_table, slot_count):
    user_count, most_blocks = block_table.shape
    live_mask = jnp.arange(most_blocks, dtype=jnp.int32)[None, :] < block_count[:, None]
    slot_hit = (
        block_table[:, :, None] == jnp.arange(slot_count, dtype=jnp.int32)[None, None, :]
    ) & live_mask[:, :, None]
    user_label = jnp.arange(user_count, dtype=jnp.int32)[:, None, None] + 1
    return jnp.sum(jnp.where(slot_hit, user_label, 0), axis=(0, 1)) - 1


def attend(queries, users, key_pairs, marks, owners):
    row_count, heads_here = (queries.shape[0], queries.shape[1])
    block_rows = min(512, row_count)
    pair_rows = key_pairs.reshape(-1, heads_here, 2, DH)
    key_rows = pair_rows[:, :, 0, :]
    value_rows = pair_rows[:, :, 1, :]
    live_mask = marks.reshape(-1, EVENTS).astype(jnp.float32)
    owner_label = owners.astype(jnp.float32)

    def one_block(packed):
        query_block, user_block = packed
        same_user = (user_block.astype(jnp.float32)[:, None] == owner_label[None, :]).astype(
            jnp.float32
        )
        weights = (same_user[:, :, None] * live_mask[None]).reshape(query_block.shape[0], -1)
        scores = jnp.einsum(
            "rhd,ehd->hre", query_block, key_rows, preferred_element_type=jnp.float32
        ) * DH ** (-0.5)
        attn_weights = (jax.nn.silu(scores) * weights[None]).astype(jnp.bfloat16)
        return jnp.einsum(
            "hre,ehd->rhd", attn_weights, value_rows, preferred_element_type=jnp.float32
        )

    result = lax.map(
        one_block, (queries.reshape(-1, block_rows, heads_here, DH), users.reshape(-1, block_rows))
    )
    return result.reshape(row_count, heads_here, DH)


def per_device(
    cand_feats, w_in, w_out, kv_cache, event_mask, block_counts, user_blocks, send_slots, cand_user
):
    row_count = cand_feats.shape[0]
    heads_here = w_out.shape[0] // DH
    projected = jnp.dot(
        lax.all_gather(cand_feats, "tp", axis=1, tiled=True),
        w_in,
        preferred_element_type=jnp.float32,
    )
    activated = jax.nn.silu(projected).reshape(row_count, heads_here, 2, DH)
    queries = activated[:, :, 0, :].astype(jnp.bfloat16)
    gates = activated[:, :, 1, :].astype(jnp.bfloat16)
    peer_count = lax.axis_size("user")
    capacity = send_slots.shape[1]
    slot_users = owner_users(block_counts, user_blocks, peer_count * capacity)
    picked = send_slots.reshape(-1)
    outgoing = kv_cache[picked].reshape(peer_count, capacity, EVENTS, kv_cache.shape[2])
    out_marks = event_mask[picked].reshape(peer_count, capacity, EVENTS).astype(jnp.bfloat16)
    arrived, arrived_marks = (
        lax.all_to_all(outgoing, "user", split_axis=0, concat_axis=0, tiled=True),
        lax.all_to_all(out_marks, "user", split_axis=0, concat_axis=0, tiled=True),
    )
    attended = attend(queries, cand_user, arrived, arrived_marks, slot_users)
    normed = (
        attended
        * lax.rsqrt(jnp.mean(attended * attended, axis=-1, keepdims=True) + norm_eps)
        * gates.astype(jnp.float32)
    )
    hidden = normed.astype(jnp.bfloat16).reshape(row_count, heads_here * DH)
    head_terms = jnp.dot(hidden, w_out, preferred_element_type=jnp.float32)
    summed = lax.psum_scatter(
        head_terms.astype(jnp.bfloat16), "tp", scatter_dimension=1, tiled=True
    ).astype(jnp.float32)
    return (cand_feats.astype(jnp.float32) + summed).astype(jnp.bfloat16)


def solution(mesh):
    in_specs = (
        P("user", "tp"),
        P(None, "tp"),
        P("tp", None),
        P("user", None, "tp"),
        P("user", None),
        P("user"),
        P("user", None),
        P("user", None),
        P("user"),
    )
    out_specs = P("user", "tp")
    return jax.shard_map(
        per_device, mesh=mesh, in_specs=in_specs, out_specs=out_specs, check_vma=False
    )
```

profile of v0, /device:TPU:1, one launch (start us, length us, event | category | flops | bytes accessed | tf_op | source)
XLA Modules:
  0.0 246.8 jit_solution(2677720347667687180)
XLA Ops:
  6.5 0.0 copy-start
  6.5 0.8 copy.22
  7.4 0.1 reshape.201
  7.5 1.4 gather_fusion.1
  8.8 0.6 convert_element_type.84
  9.5 11.9 %all-to-all-start.1 = ((bf16[32,2,128]{2,1,0:T(2,128)(2,1)}), bf16[32,2,128]{2,1,0:T(2,128)(2,1)S(1)}, u32[]{:S(2)}, u32[]{:S(2)}) async-start(bf16[32,2,128]{2,1,0:T(2,128)(2,1)} %bitcast.14), calls=%async_computation.1 | async-start | bytes 32768 | tf_op jit(solution)/shard_map/all_to_all | solution.py:73
  21.3 5.0 %gather_fusion = bf16[64,128,256]{2,1,0:T(8,128)(2,1)} fusion(bf16[64,128,256]{2,1,0:T(8,128)(2,1)} %param.14, s32[1024]{0:T(1024)S(1)} %pad_clamp_fusion), kind=kCustom, calls=%fused_computation | custom fusion | bytes 8388864 | tf_op jit(solution)/shard_map/gather | solution.py:69
  26.3 3.5 %all-to-all-done.1 = bf16[32,2,128]{2,1,0:T(2,128)(2,1)S(1)} async-done(((bf16[32,2,128]{2,1,0:T(2,128)(2,1)}), bf16[32,2,128]{2,1,0:T(2,128)(2,1)S(1)}, u32[]{:S(2)}, u32[]{:S(2)}) %all-to-all-start.1) | async-done | bytes 16416 | tf_op jit(solution)/shard_map/all_to_all | solution.py:73
  29.8 0.0 copy-start.5
  29.8 0.0 copy-start.6
  29.8 0.0 copy-start.4
  29.8 6.0 %all-to-all-start = ((bf16[32,2,128,256]{3,2,1,0:T(8,128)(2,1)}), bf16[32,2,128,256]{3,2,1,0:T(8,128)(2,1)}, u32[]{:S(2)}, u32[]{:S(2)}) async-start(bf16[32,2,128,256]{3,2,1,0:T(8,128)(2,1)} %bitcast.92), calls=%async_computation | async-start | bytes 8388608 | tf_op jit(solution)/shard_map/all_to_all | solution.py:72
  35.8 0.0 all-gather.2.cloned.1.call-start
  35.9 0.7 all-gather.2.cloned.1.call-update
  36.5 0.0 reduce-scatter.4.cloned.1.call-start
  36.6 0.0 copy-done.5
  36.6 0.0 copy-done.6
  36.6 0.1 iota_compare_fusion.1
  36.7 0.0 copy-done.4
  36.7 0.1 select_reduce_fusion
  36.8 34.1 %all-gather.2.cloned.1.call-done = bf16[1024,1024]{1,0:T(8,128)(2,1)} async-done(((bf16[1024,128]{1,0:T(8,128)(2,1)}), bf16[1024,1024]{1,0:T(8,128)(2,1)}) %all-gather.2.cloned.1.call-update) | async-done | bytes 2097168 | tf_op jit(solution)/shard_map/all_gather | solution.py:58
  70.9 0.0 copy-done
  70.9 2.5 %multiply_convert_fusion = bf16[1024,256]{0,1:T(8,128)(2,1)S(1)} fusion(bf16[1024,1024]{1,0:T(8,128)(2,1)} %all-gather.2.cloned.1.call-done, bf16[1024,256]{1,0:T(8,128)(2,1)S(1)} %copy-done), kind=kOutput, calls=%fused_computation.20 | convolution fusion | flops 538181632 | bytes 3145728 | tf_op jit(solution)/shard_map/dot_general | solution.py:57
  73.4 0.0 copy-start.2
  73.5 0.8 copy-done.2
  74.3 0.8 copy.29
  75.1 52.7 %all-to-all-done = bf16[32,2,128,256]{3,2,1,0:T(8,128)(2,1)} async-done(((bf16[32,2,128,256]{3,2,1,0:T(8,128)(2,1)}), bf16[32,2,128,256]{3,2,1,0:T(8,128)(2,1)}, u32[]{:S(2)}, u32[]{:S(2)}) %all-to-all-start) | async-done | bytes 4194336 | tf_op jit(solution)/shard_map/all_to_all | solution.py:72
  127.8 7.0 %reshape.203 = bf16[8192,1,2,128]{3,2,0,1:T(2,128)(2,1)} reshape(bf16[32,2,128,256]{3,2,1,0:T(8,128)(2,1)} %all-to-all-done) | data formatting | bytes 8388608 | tf_op jit(solution)/shard_map/reshape | solution.py:26
  134.8 8.9 %fusion.29 = (bf16[8192,1,1,128]{3,2,0,1:T(2,128)(2,1)S(1)}, bf16[8192,1,1,128]{3,2,0,1:T(2,128)(2,1)S(1)}) fusion(bf16[8192,1,2,128]{3,2,0,1:T(2,128)(2,1)} %reshape.203), kind=kLoop, calls=%fused_computation.37 | loop fusion | bytes 8388608 | tf_op jit(solution)/shard_map/slice | solution.py:28
  143.7 1.9 copy_bitcast_fusion
  145.6 53.2 %while.10 = (s32[]{:T(128)}, f32[2,512,1,128]{3,1,2,0:T(8,128)S(1)}, bf16[2,512,1,128]{3,1,2,0:T(8,128)(2,1)}, bf16[8192,1,128]{2,0,1:T(8,128)(2,1)}, s32[2,512]...) while((s32[]{:T(128)}, ...), condition=%wide.region_2.3_spmd, body=%wide.region_1.2_spmd.sunk | while | flops 2181104128 | bytes 38444384 | solution.py:46
  145.6 0.1 compare_convert_fusion.2
  145.7 7.0 %mul.127 = f32[512,64,128]{2,1,0:T(8,128)} broadcast(f32[512,64]{1,0:T(8,128)S(1)} %compare_convert_fusion.2), dimensions={0,1} | broadcast | bytes 16908288 | tf_op jit(solution)/shard_map/while/body/eval_jaxpr/mul | solution.py:37
  152.7 19.4 %fusion.40 = f32[2,512,1,128]{3,1,2,0:T(8,128)S(1)} fusion(f32[2,512,1,128]{3,1,2,0:T(8,128)S(1)} %get-tuple-element.151, s32[]{:T(128)} %get-tuple-element.150, bf16[8192,1,128]{2,0,1:T(8,128)(2,1)S(1)} %get-tuple-element.166, f32[64,8,64,128]{3,2,1,0:T(8,128)} %bitcast.91, f32[8192]{0:T(1024)S(1)} %bitcast.101, ...), kind=kOutput, calls=%fused_computation.9.clone.1 | convolution fusion | flops 2181038080 | bytes 21398528 | tf_op jit(solution)/shard_map/while/body/eval_jaxpr/hre,ehd->rhd/dot_general | solution.py:42
  172.2 0.1 compare_convert_fusion.2
  172.3 7.0 %mul.127 = f32[512,64,128]{2,1,0:T(8,128)} broadcast(f32[512,64]{1,0:T(8,128)S(1)} %compare_convert_fusion.2), dimensions={0,1} | broadcast | bytes 16908288 | tf_op jit(solution)/shard_map/while/body/eval_jaxpr/mul | solution.py:37
  179.4 19.4 %fusion.40 = f32[2,512,1,128]{3,1,2,0:T(8,128)S(1)} fusion(f32[2,512,1,128]{3,1,2,0:T(8,128)S(1)} %get-tuple-element.151, s32[]{:T(128)} %get-tuple-element.150, bf16[8192,1,128]{2,0,1:T(8,128)(2,1)S(1)} %get-tuple-element.166, f32[64,8,64,128]{3,2,1,0:T(8,128)} %bitcast.91, f32[8192]{0:T(1024)S(1)} %bitcast.101, ...), kind=kOutput, calls=%fused_computation.9.clone.1 | convolution fusion | flops 2181038080 | bytes 21398528 | tf_op jit(solution)/shard_map/while/body/eval_jaxpr/hre,ehd->rhd/dot_general | solution.py:42
  198.8 0.2 multiply_reduce_fusion
  199.0 0.2 copy.24
  199.3 0.0 copy-done.3
  199.3 1.7 convolution_convert_fusion
  201.0 0.0 copy-start.1
  201.0 2.6 %copy.25 = bf16[1024,1024]{0,1:T(8,128)(2,1)} copy(bf16[1024,1024]{1,0:T(8,128)(2,1)S(1)} %convolution_convert_fusion) | data formatting | bytes 4194304
  203.6 0.0 reduce-scatter.4.cloned.1.call-update
  203.6 34.5 %reduce-scatter.4.cloned.1.call-done = bf16[128,1024]{1,0:T(8,128)(2,1)} async-done(((bf16[1024,1024]{1,0:T(8,128)(2,1)}), bf16[128,1024]{1,0:T(8,128)(2,1)}) %reduce-scatter.4.cloned.1.call-update) | async-done | bytes 262160
  238.0 1.1 copy.26
  239.2 0.0 copy-done.1
  239.2 0.8 add_convert_fusion
  (13 shorter events, 0.1 us)
Async XLA Ops:
  6.5 64.4 %copy-start = (bf16[1024,256]{1,0:T(8,128)(2,1)S(1)}, bf16[1024,256]{1,0:T(8,128)(2,1)}, u32[]{:S(2)}) copy-start(bf16[1024,256]{1,0:T(8,128)(2,1)} %param.12) | copy-start | bytes 1572868
  9.5 20.4 %all-to-all-start.1 = ((bf16[32,2,128]{2,1,0:T(2,128)(2,1)}), bf16[32,2,128]{2,1,0:T(2,128)(2,1)S(1)}, u32[]{:S(2)}, u32[]{:S(2)}) async-start(bf16[32,2,128]{2,1,0:T(2,128)(2,1)} %bitcast.14), calls=%async_computation.1 | async-start | bytes 32768 | tf_op jit(solution)/shard_map/all_to_all | solution.py:73
  29.8 6.8 %copy-start.5 = (s32[1024]{0:T(1024)S(1)}, s32[1024]{0:T(1024)}, u32[]{:S(2)}) copy-start(s32[1024]{0:T(1024)} %param.19) | copy-start | bytes 12292
  29.8 6.8 %copy-start.6 = (s32[8]{0:T(128)S(1)}, s32[8]{0:T(128)}, u32[]{:S(2)}) copy-start(s32[8]{0:T(128)} %param.16) | copy-start | bytes 100
  29.8 6.9 %copy-start.4 = (s32[8,8]{1,0:T(8,128)S(1)}, s32[8,8]{1,0:T(8,128)}, u32[]{:S(2)}) copy-start(s32[8,8]{1,0:T(8,128)} %param.17) | copy-start | bytes 772
  29.8 98.0 %all-to-all-start = ((bf16[32,2,128,256]{3,2,1,0:T(8,128)(2,1)}), bf16[32,2,128,256]{3,2,1,0:T(8,128)(2,1)}, u32[]{:S(2)}, u32[]{:S(2)}) async-start(bf16[32,2,128,256]{3,2,1,0:T(8,128)(2,1)} %bitcast.92), calls=%async_computation | async-start | bytes 8388608 | tf_op jit(solution)/shard_map/all_to_all | solution.py:72
  35.8 35.1 %all-gather.2.cloned.1.call-start = ((), (), s32[]{:S(2)}) async-start(), calls=%async_computation.3 | async-start | bytes 2359296 | tf_op jit(solution)/shard_map/all_gather | solution.py:58
  36.5 201.5 %reduce-scatter.4.cloned.1.call-start = ((), (), s32[]{:S(2)}) async-start(), calls=%async_computation.4 | async-start | bytes 2359296
  73.4 0.8 copy-start.2
  145.6 53.7 %copy-start.3 = (bf16[128,1024]{1,0:T(8,128)(2,1)S(1)}, bf16[128,1024]{1,0:T(8,128)(2,1)}, u32[]{:S(2)}) copy-start(bf16[128,1024]{1,0:T(8,128)(2,1)} %param.13) | copy-start | bytes 786436
  201.0 38.2 %copy-start.1 = (bf16[1024,128]{1,0:T(8,128)(2,1)S(1)}, bf16[1024,128]{1,0:T(8,128)(2,1)}, u32[]{:S(2)}) copy-start(bf16[1024,128]{1,0:T(8,128)(2,1)} %param.11) | copy-start | bytes 786436
Sparse Core Ops, SparseCore 0:
  38.5 32.4 all-gather.1
  203.7 34.3 reduce-scatter.3
where the time goes:
time: 249 us; the launch traced here: 247 us
  waiting for transfers between devices  126 us (51%)
  local copies, waits for them, and re-layouts  44.6 us (18%)
  matrix products  43 us (17%)
  starting transfers between devices  17.9 us (7%)
  between operations  13.6 us (5%)
    all_to_all x1, waiting for transfers between devices, per_device(): lax.all_to_all(outgoing, 'user', split_axis=0, concat_axis=0, tiled=True)  52.7 us
    dot_general x2, matrix products, one_block(): jnp.einsum('hre,ehd->rhd', attn_weights, value_rows, preferred_element_ty...  38.9 us
    unnamed x3, waiting for transfers between devices  35.2 us
    all_gather x1, waiting for transfers between devices, per_device(): lax.all_gather(cand_feats, 'tp', axis=1, tiled=True)  34.1 us
    mul x2, local copies, waits for them, and re-layouts, one_block(): same_user[:, :, None] * live_mask[None]  14 us
    all_to_all x1, starting transfers between devices, per_device(): lax.all_to_all(out_marks, 'user', split_axis=0, concat_axis=0, tiled=True)  11.9 us
    slice x1, local copies, waits for them, and re-layouts, attend(): value_rows = pair_rows[:, :, 1, :]  8.89 us
    unnamed x20, local copies, waits for them, and re-layouts  8.03 us
  transfers between devices with their start and end apart: 4, of which 4 were waited for; matrix products, arithmetic and copies ran while one was open for 3% of the time, Pallas kernels for 0%

commit v1 on v0

v1 whole, which is shorter than its diff:
```python
import functools

import jax
import jax.numpy as jnp
from jax import lax
from jax.experimental import pallas as pl
from jax.experimental.pallas import tpu as pltpu
from jax.sharding import PartitionSpec as P

DH = 128
EVENTS = 128
CAP = 2
CORES = 2
Z_SIZE = 8
norm_eps = 1e-06
FAR = -float(2**30)
HALF_SCALE = 0.5 * DH**-0.5
MESH = pl.DeviceIdType.MESH


def silu(v):
    x = 0.5 * v
    return x + x * jnp.tanh(x)


def kernel(
    dims,
    slots_ref,
    info_ref,
    mask_ref,
    kv_hbm,
    feats_hbm,
    w_in_hbm,
    w_out_hbm,
    out_ref,
    kv_v,
    snd,
    kvr,
    feats,
    w_in_v,
    w_out_v,
    w_out_all,
    info_all,
    qs,
    gates,
    onehot,
    parts,
    incoming,
    att,
    hid,
    loc_sem,
    x_ss,
    x_rs,
    info_ss,
    info_rs,
    f_ss,
    f_rs,
    h_ss,
    h_rs,
    w_ss,
    w_rs,
    q_ss,
    q_rs,
    p_ss,
    p_rs,
):
    nz, nx, ny = dims
    far = nz // 2
    half = feats.shape[2]
    n_tp = ny * CORES
    n_blk = nx * CAP
    me_u = lax.axis_index("user")
    me_t = lax.axis_index("tp")
    z, x = me_u // nx, me_u % nx
    y, core = me_t // CORES, me_t % CORES

    def at_z(d):
        return ((z + d + nz) % nz * nx + x, me_t)

    def at_x(j):
        return (z * nx + (x + j) % nx, me_t)

    def at_t(t):
        return (me_u, t)

    def rc(src, dst, ss, rs, dev):
        return pltpu.make_async_remote_copy(
            src_ref=src, dst_ref=dst, send_sem=ss, recv_sem=rs,
            device_id=dev, device_id_type=MESH,
        )

    kv_load = pltpu.make_async_copy(kv_hbm, kv_v, loc_sem.at[0])
    wi_load = pltpu.make_async_copy(w_in_hbm, w_in_v, loc_sem.at[1])
    wo_load = pltpu.make_async_copy(w_out_hbm, w_out_v, loc_sem.at[2])
    f_loads = [
        pltpu.make_async_copy(feats_hbm.at[h], feats.at[me_t, h], loc_sem.at[3 + h])
        for h in range(2)
    ]
    for load in f_loads:
        load.start()
    kv_load.start()
    wi_load.start()
    wo_load.start()

    barrier = pltpu.get_barrier_semaphore()
    peers = [at_z(d) for d in range(1, nz)]
    peers += [at_x(j) for j in range(1, nx)]
    peers += [at_t((me_t + j) % n_tp) for j in range(1, n_tp)]
    for dev in peers:
        pl.semaphore_signal(barrier, inc=1, device_id=dev, device_id_type=MESH)
    onehot[...] = jnp.zeros_like(onehot)
    info_all[0] = info_ref[z]
    pl.semaphore_wait(barrier, len(peers))

    sends = []

    def go(copy):
        copy.start()
        sends.append(copy)

    partner = y * CORES + 1 - core

    def y_src(j, c):
        return (y - j + ny) % ny * CORES + c

    def y_send(buf, h, ss, rs):
        own = buf.at[me_t, h]
        for j in range(1, ny):
            go(rc(own, own, ss.at[h, j], rs.at[h, j], at_t((y + j) % ny * CORES + core)))
        go(rc(own, own, ss.at[h, 0], rs.at[h, 0], at_t(partner)))

    def y_forward(buf, h, ss, rs):
        for j in range(1, ny):
            got = buf.at[y_src(j, core), h]
            rc(got, got, ss.at[h, j], rs.at[h, j], at_t(partner)).wait_recv()
            k = ny - 1 + j
            go(rc(got, got, ss.at[h, k], rs.at[h, k], at_t(partner)))

    def y_wait(buf, h, ss, rs):
        for j in range(ny):
            k = 0 if j == 0 else ny - 1 + j
            got = buf.at[y_src(j, 1 - core), h]
            rc(got, got, ss.at[h, k], rs.at[h, k], at_t(partner)).wait_recv()

    for h in range(2):
        f_loads[h].wait()
        y_send(feats, h, f_ss, f_rs)
    for d in range(1, nz):
        go(rc(info_ref.at[(z + d) % nz], info_all.at[d], info_ss.at[d], info_rs.at[d], at_z(d)))

    def prepare(k):
        ranker = (z - k + nz) % nz * nx

        def one(i, carry):
            j, c = i // CAP, i % CAP
            slot = slots_ref[ranker + (x + j) % nx, c]
            block = kv_v[slot]
            live = mask_ref[slot].astype(jnp.float32).astype(jnp.bfloat16)
            snd[k, j, c, :, 0:DH] = block[:, 0:DH]
            snd[k, j, c, :, DH:] = block[:, DH:].T * live
            return carry

        lax.fori_loop(0, n_blk, one, 0)
        for j in range(1, nx):
            go(rc(snd.at[k, j], kvr.at[k, j], x_ss.at[k, j], x_rs.at[k, j], at_x(j)))

    def q_slot(way, d):
        return way * far + d if d else 0

    def project(h):
        rows = jnp.concatenate([feats[t, h] for t in range(n_tp)], axis=1)
        act = silu(jnp.dot(rows, w_in_v[...], preferred_element_type=jnp.float32))
        qs[0, h] = act[:, 0:DH].T.astype(jnp.bfloat16)
        gates[h] = act[:, DH:].astype(jnp.bfloat16)

    def q_copy(way, d, h):
        return rc(
            qs.at[q_slot(way, d - 1), h], qs.at[q_slot(way, d), h],
            q_ss.at[way, d, h], q_rs.at[way, d, h], at_z(1 if way == 0 else -1),
        )

    def q_ways(d, h):
        return [w for w in range(2) if d < far or w == h] if d <= far else []

    order = [far]
    for d in range(far - 1, 0, -1):
        order += [d, nz - d]
    order += [0]

    kv_load.wait()
    todo = list(order)
    prepare(todo.pop(0))
    y_forward(feats, 0, f_ss, f_rs)
    if todo:
        prepare(todo.pop(0))
    y_forward(feats, 1, f_ss, f_rs)
    wi_load.wait()
    y_wait(feats, 0, f_ss, f_rs)
    project(0)
    for way in q_ways(1, 0):
        go(q_copy(way, 1, 0))
    y_wait(feats, 1, f_ss, f_rs)
    project(1)
    for way in q_ways(1, 1):
        go(q_copy(way, 1, 1))
    wo_load.wait()
    w_out_all[me_t] = w_out_v[:, pl.ds(pl.multiple_of(me_t * DH, DH), DH)]
    for j in range(1, n_tp):
        t = (me_t + j) % n_tp
        cols = pl.ds(pl.multiple_of(t * DH, DH), DH)
        go(rc(w_out_v.at[:, cols], w_out_all.at[me_t], w_ss.at[j], w_rs.at[j], at_t(t)))
    for d in range(1, far):
        for h in range(2):
            if todo:
                prepare(todo.pop(0))
            for way in q_ways(d, h):
                q_copy(way, d, h).wait_recv()
                if way in q_ways(d + 1, h):
                    go(q_copy(way, d + 1, h))
    while todo:
        prepare(todo.pop(0))

    def p_copy(way, d, h):
        to = (z + 2 * way - 1 + nz) % nz * nx + x
        return rc(
            parts.at[way, d - 1, h], incoming.at[way, d - 1, h],
            p_ss.at[way, d - 1, h], p_rs.at[way, d - 1, h], (to, me_t),
        )

    def attend(k, q, h):
        user = lax.broadcasted_iota(jnp.int32, (16, DH), 0).astype(jnp.float32)
        for i in range(half // DH):
            row = info_all[k, pl.ds(h * (half // DH) + i, 1), :]
            onehot[0:16, i * DH : (i + 1) * DH] = jnp.where(row == user, 1.0, 0.0).astype(jnp.bfloat16)
        keys, values = [], []
        for j in range(nx):
            for c in range(CAP):
                block = snd[k, 0, c] if j == 0 else kvr[k, j, c]
                b = (x - j + nx) % nx * CAP + c
                ext = info_all[k, pl.ds(8 + b, 1), :].astype(jnp.bfloat16)
                ext = jnp.broadcast_to(ext, (EVENTS, DH))
                keys.append(jnp.concatenate([block[:, 0:DH], ext], axis=1))
                values.append(block[:, DH:])
        rhs = jnp.concatenate([qs[q, h], onehot[...]], axis=0)
        v = HALF_SCALE * jnp.dot(
            jnp.concatenate(keys, axis=0), rhs, preferred_element_type=jnp.float32
        )
        w = (v + v * jnp.tanh(v)).astype(jnp.bfloat16)
        return jnp.dot(jnp.concatenate(values, axis=1), w, preferred_element_type=jnp.float32)

    def wait_blocks(k):
        for j in range(1, nx):
            rc(snd.at[k, j], kvr.at[k, j], x_ss.at[k, j], x_rs.at[k, j], at_x(j)).wait_recv()

    def wait_info(k):
        rc(info_ref.at[0], info_all.at[k], info_ss.at[k], info_rs.at[k], at_z(1)).wait_recv()

    def one_task(i, carry):
        d = far - (i + 2) // 4
        r = (i + 2) % 4
        at_far = d // far
        way = r % 2
        h = (1 - at_far) * (r // 2) + at_far * (r % 2)
        k = (d + way * (nz - 2 * d)) % nz
        first = (1 - at_far) * (r // 2) + at_far * way

        @pl.when(jnp.logical_and(first == 0, d > 0))
        def _():
            wait_blocks(k)
            wait_info(k)

        @pl.when(jnp.logical_and(r == 0, d == 0))
        def _():
            wait_blocks(k)

        @pl.when(d == far)
        def _():
            rc(
                qs.at[0, h], qs.at[way * far + d, h], q_ss.at[way, d, h], q_rs.at[way, d, h], at_z(1)
            ).wait_recv()

        own = (d + far - 1) // far
        hh = own * h + (1 - own) * way
        total = attend(k, own * (way * far + d), hh)

        @pl.when(d == 0)
        def _():
            att[hh] = total

        @pl.when(jnp.logical_and(d > 0, jnp.logical_or(d == far, jnp.logical_and(d == far - 1, h != way))))
        def _():
            parts[way, d - 1, h] = total.astype(jnp.bfloat16)

        @pl.when(jnp.logical_and(d > 0, jnp.logical_or(d < far - 1, jnp.logical_and(d == far - 1, h == way))))
        def _():
            p_copy(way, d + 1, h).wait_recv()
            parts[way, d - 1, h] = (total + incoming[way, d, h].astype(jnp.float32)).astype(jnp.bfloat16)

        @pl.when(d > 0)
        def _():
            p_copy(way, d, h).start()

        return carry

    lax.fori_loop(0, 4 * far, one_task, 0)

    for h in range(2):
        total = att[h]
        for way in q_ways(1, h):
            p_copy(way, 1, h).wait_recv()
            total = total + incoming[way, 0, h].astype(jnp.float32)
        inv = lax.rsqrt(jnp.mean(total * total, axis=0, keepdims=True) + norm_eps)
        normed = (total * inv).T * gates[h].astype(jnp.float32)
        hid[me_t, h] = normed.astype(jnp.bfloat16)
        y_send(hid, h, h_ss, h_rs)
    for j in range(1, n_tp):
        t = (me_t - j + n_tp) % n_tp
        rc(w_out_all.at[t], w_out_all.at[t], w_ss.at[j], w_rs.at[j], at_t(t)).wait_recv()
    y_forward(hid, 0, h_ss, h_rs)
    y_forward(hid, 1, h_ss, h_rs)
    w_all = jnp.concatenate([w_out_all[t] for t in range(n_tp)], axis=0)
    for h in range(2):
        y_wait(hid, h, h_ss, h_rs)
        rows = jnp.concatenate([hid[t, h] for t in range(n_tp)], axis=1)
        mixed = jnp.dot(rows, w_all, preferred_element_type=jnp.float32)
        out_ref[h] = (feats[me_t, h].astype(jnp.float32) + mixed).astype(jnp.bfloat16)
    for copy in sends:
        copy.wait_send()
    for d in range(1, far + 1):
        for h in range(2):
            for way in q_ways(d, h):
                p_copy(way, d, h).wait_send()


def per_device(
    nz, cand_feats, w_in, w_out, kv_cache, event_mask, block_counts, user_blocks, send_slots, cand_user
):
    rows = cand_feats.shape[0]
    half = rows // 2
    nx = lax.axis_size("user") // nz
    n_tp = lax.axis_size("tp")
    ny = n_tp // CORES
    far = nz // 2
    users, most = user_blocks.shape
    n_slots = nz * nx * CAP
    valid = jnp.arange(most, dtype=jnp.int32)[None, :] < block_counts[:, None]
    hit = (user_blocks[None] == jnp.arange(n_slots, dtype=jnp.int32)[:, None, None]) & valid[None]
    ext = jnp.where(jnp.any(hit, axis=2), 0.0, FAR).astype(jnp.float32)
    ext = jnp.pad(ext, ((0, 0), (0, DH - users))).reshape(nz, nx * CAP, DH)
    ext = jnp.pad(ext, ((0, 0), (0, 8 - nx * CAP), (0, 0)))
    who = cand_user.astype(jnp.float32).reshape(-1, DH)
    who = jnp.pad(who, ((0, 8 - who.shape[0]), (0, 0)))
    info = jnp.concatenate([jnp.broadcast_to(who[None], (nz, 8, DH)), ext], axis=1)

    bf16, f32 = jnp.bfloat16, jnp.float32
    dma = pltpu.SemaphoreType.DMA
    any_spec = pl.BlockSpec(memory_space=pl.ANY)
    vmem = pl.BlockSpec(memory_space=pltpu.VMEM)
    out = pl.pallas_call(
        functools.partial(kernel, (nz, nx, ny)),
        out_shape=jax.ShapeDtypeStruct((2, half, DH), bf16),
        in_specs=[pl.BlockSpec(memory_space=pltpu.SMEM), vmem, vmem] + [any_spec] * 4,
        out_specs=vmem,
        scratch_shapes=[
            pltpu.VMEM(kv_cache.shape, bf16),
            pltpu.VMEM((nz, nx, CAP, EVENTS, 2 * DH), bf16),
            pltpu.VMEM((nz, nx, CAP, EVENTS, 2 * DH), bf16),
            pltpu.VMEM((n_tp, 2, half, DH), bf16),
            pltpu.VMEM(w_in.shape, bf16),
            pltpu.VMEM(w_out.shape, bf16),
            pltpu.VMEM((n_tp, DH, DH), bf16),
            pltpu.VMEM((nz, 16, DH), f32),
            pltpu.VMEM((2 * far + 1, 2, DH, half), bf16),
            pltpu.VMEM((2, half, DH), bf16),
            pltpu.VMEM((DH, half), bf16),
            pltpu.VMEM((2, far, 2, DH, half), bf16),
            pltpu.VMEM((2, far, 2, DH, half), bf16),
            pltpu.VMEM((2, DH, half), f32),
            pltpu.VMEM((n_tp, 2, half, DH), bf16),
            dma((5,)),
            dma((nz, nx)),
            dma((nz, nx)),
            dma((nz,)),
            dma((nz,)),
            dma((2, 2 * ny - 1)),
            dma((2, 2 * ny - 1)),
            dma((2, 2 * ny - 1)),
            dma((2, 2 * ny - 1)),
            dma((n_tp,)),
            dma((n_tp,)),
            dma((2, far + 1, 2)),
            dma((2, far + 1, 2)),
            dma((2, far, 2)),
            dma((2, far, 2)),
        ],
        compiler_params=pltpu.CompilerParams(
            collective_id=0, has_side_effects=True, vmem_limit_bytes=52 * 2**20
        ),
        name="score",
    )(
        send_slots,
        info,
        event_mask.reshape(-1, 1, EVENTS),
        kv_cache,
        cand_feats.reshape(2, half, DH),
        w_in,
        w_out,
    )
    return out.reshape(rows, DH)


def solution(mesh):
    in_specs = (
        P("user", "tp"),
        P(None, "tp"),
        P("tp", None),
        P("user", None, "tp"),
        P("user", None),
        P("user"),
        P("user", None),
        P("user", None),
        P("user"),
    )
    return jax.shard_map(
        functools.partial(per_device, Z_SIZE),
        mesh=mesh,
        in_specs=in_specs,
        out_specs=P("user", "tp"),
        check_vma=False,
    )
```

time: 249 us -> 93.7 us (0.38)
  waiting for transfers between devices: 126 us -> 0 us
  Pallas kernels: 0 us -> 85.9 us
  matrix products: 43 us -> 0 us
  local copies, waits for them, and re-layouts: 44.6 us -> 5.25 us
  starting transfers between devices: 17.9 us -> 0 us
  between operations: 13.6 us -> 0.03 us
    pallas_call x0 -> x1, Pallas kernels: none -> 85.9 us  [per_device(): pl.pallas_call(functools.partial(kernel, (nz, nx, ny)), out_shape=jax.Sha...]
    all_to_all x2 -> x0, waiting for transfers between devices: 56.2 us -> none  [the longest x1 52.7 us: per_device(): lax.all_to_all(outgoing, 'user', split_axis=0, concat_axis=0, tiled=True)]
    dot_general x4 -> x0, matrix products: 43 us -> none  [the longest x2 38.9 us: one_block(): jnp.einsum('hre,ehd->rhd', attn_weights, value_rows, preferred_element_ty...]
    unnamed x3 -> x0, waiting for transfers between devices: 35.2 us -> none
    all_gather x1 -> x0, waiting for transfers between devices: 34.1 us -> none  [per_device(): lax.all_gather(cand_feats, 'tp', axis=1, tiled=True)]
    all_to_all x2 -> x0, starting transfers between devices: 17.8 us -> none  [the longest x1 11.9 us: per_device(): lax.all_to_all(out_marks, 'user', split_axis=0, concat_axis=0, tiled=True)]
    mul x2 -> x0, local copies, waits for them, and re-layouts: 14 us -> none  [one_block(): same_user[:, :, None] * live_mask[None]]
    slice x2 -> x0, local copies, waits for them, and re-layouts: 8.91 us -> none  [the longest x1 8.89 us: attend(): value_rows = pair_rows[:, :, 1, :]]
  transfers between devices with their start and end apart: 4 -> 0, of which waited for: 4 -> 0; matrix products, arithmetic and copies ran while one was open for 3% -> 0% of each run, Pallas kernels for 0% -> 0%
where the time goes in v1:
time: 93.7 us; the launch traced here: 93.4 us
  Pallas kernels  85.9 us (92%)
  local copies, waits for them, and re-layouts  5.25 us (6%)
  other arithmetic  2.21 us (2%)
    pallas_call x1, Pallas kernels, per_device(): pl.pallas_call(functools.partial(kernel, (nz, nx, ny)), out_shape=jax.Sha...  85.9 us
    unnamed x11, local copies, waits for them, and re-layouts  5.24 us

profile of v1, /device:TPU:1, one launch (start us, length us, event | category | flops | bytes accessed | tf_op | source)
XLA Modules:
  0.0 93.4 jit_solution(5580400743011046646)
XLA Ops:
  0.0 0.7 iota_compare_fusion.1
  0.7 0.8 fusion.1
  1.5 0.7 convert_bitcast_fusion
  2.2 0.8 copy.12.slots_ref
  3.0 0.1 copy.13
  3.1 0.0 copy-start
  3.1 1.0 %copy-done = bf16[1024,256]{1,0:T(8,128)(2,1)S(1)} copy-done((bf16[1024,256]{1,0:T(8,128)(2,1)S(1)}, bf16[1024,256]{1,0:T(8,128)(2,1)}, u32[]{:S(2)}) %copy-start) | copy-done | bytes 524312
  4.1 0.0 copy-start.1
  4.1 0.9 %copy-done.1 = bf16[1024,128]{1,0:T(8,128)(2,1)S(1)} copy-done((bf16[1024,128]{1,0:T(8,128)(2,1)S(1)}, bf16[1024,128]{1,0:T(8,128)(2,1)}, u32[]{:S(2)}) %copy-start.1) | copy-done | bytes 262168
  5.1 0.0 copy-start.2
  5.1 0.9 %copy-done.2 = bf16[128,1024]{1,0:T(8,128)(2,1)S(1)} copy-done((bf16[128,1024]{1,0:T(8,128)(2,1)S(1)}, bf16[128,1024]{1,0:T(8,128)(2,1)}, u32[]{:S(2)}) %copy-start.2) | copy-done | bytes 262168
  6.0 0.0 copy-start.3
  6.0 0.8 copy-done.3
  6.8 85.9 %score.1 = bf16[2,512,128]{2,1,0:T(8,128)(2,1)S(1)} custom-call(s32[32,2]{1,0:T(8,128)S(1)} %copy.12.slots_ref, f32[8,16,128]{2,1,0:T(8,128)S(1)} %pad_maximum_fusion.info_ref, s32[64,1,128]{2,1,0:T(1,128)S(1)} %bitcast.9, bf16[64,128,256]{2,1,0:T(8,128)(2,1)} %kv_hbm.1, bf16[2,512,128]{2,1,0:T(8,128)(2,1)S(1)} %bitcast.8, bf16[1024,256]{1,0:T(8,128)(2,1)S(1)} %copy-done, ...), custom_call_target="tpu_custom_call" | custom-call | tf_op jit(solution)/shard_map/score/pallas_call | solution.py:359
  92.7 0.7 copy.15
  (4 shorter events, 0.0 us)
Async XLA Ops:
  3.1 1.0 %copy-start = (bf16[1024,256]{1,0:T(8,128)(2,1)S(1)}, bf16[1024,256]{1,0:T(8,128)(2,1)}, u32[]{:S(2)}) copy-start(bf16[1024,256]{1,0:T(8,128)(2,1)} %w_in_hbm.1) | copy-start | bytes 1572868
  4.1 0.9 %copy-start.1 = (bf16[1024,128]{1,0:T(8,128)(2,1)S(1)}, bf16[1024,128]{1,0:T(8,128)(2,1)}, u32[]{:S(2)}) copy-start(bf16[1024,128]{1,0:T(8,128)(2,1)} %param.9) | copy-start | bytes 786436
  5.1 0.9 %copy-start.2 = (bf16[128,1024]{1,0:T(8,128)(2,1)S(1)}, bf16[128,1024]{1,0:T(8,128)(2,1)}, u32[]{:S(2)}) copy-start(bf16[128,1024]{1,0:T(8,128)(2,1)} %w_out_hbm.1) | copy-start | bytes 786436
  6.0 0.8 copy-start.3

commit v2 on v0

v2 whole, which is shorter than its diff:
```python
import functools

import jax
import jax.numpy as jnp
from jax import lax
from jax.experimental import pallas as pl
from jax.experimental.pallas import tpu as pltpu
from jax.sharding import PartitionSpec as P

DH = 128
EVENTS = 128
CAP = 2
CORES = 2
Z_SIZE = 8
CHUNKS = 4
WINDOW = 3
norm_eps = 1e-06
FAR = -float(2**30)
HALF_SCALE = 0.5 * DH**-0.5
MESH = pl.DeviceIdType.MESH


def silu(v):
    x = 0.5 * v
    return x + x * jnp.tanh(x)


def kernel(
    dims,
    slots_ref,
    counts_ref,
    blocks_ref,
    who_hbm,
    mask_hbm,
    kv_hbm,
    feats_hbm,
    w_in_hbm,
    w_out_hbm,
    out_ref,
    who_v,
    mask_v,
    kv_v,
    snd,
    kvr,
    feats,
    w_in_v,
    w_out_v,
    w_out_all,
    ext_v,
    info_out,
    info_all,
    qs,
    gates,
    onehot,
    parts,
    incoming,
    hid,
    loc_sem,
    x_ss,
    x_rs,
    info_ss,
    info_rs,
    f_ss,
    f_rs,
    h_ss,
    h_rs,
    w_ss,
    w_rs,
    q_ss,
    q_rs,
    p_ss,
    p_rs,
):
    nz, nx, ny = dims
    far = nz // 2
    win = WINDOW
    rows = feats.shape[2]
    n_tp = ny * CORES
    n_blk = nx * CAP
    users, most = blocks_ref.shape
    me_u = lax.axis_index("user")
    me_t = lax.axis_index("tp")
    z, x = me_u // nx, me_u % nx
    y, core = me_t // CORES, me_t % CORES

    def at_z(d):
        return ((z + d + nz) % nz * nx + x, me_t)

    def at_x(j):
        return (z * nx + (x + j) % nx, me_t)

    def at_t(t):
        return (me_u, t)

    def rc(src, dst, ss, rs, dev):
        return pltpu.make_async_remote_copy(
            src_ref=src, dst_ref=dst, send_sem=ss, recv_sem=rs,
            device_id=dev, device_id_type=MESH,
        )

    f_load = pltpu.make_async_copy(feats_hbm, feats.at[me_t], loc_sem.at[0])
    kv_load = pltpu.make_async_copy(kv_hbm, kv_v, loc_sem.at[1])
    wi_load = pltpu.make_async_copy(w_in_hbm, w_in_v, loc_sem.at[2])
    wo_load = pltpu.make_async_copy(w_out_hbm, w_out_v, loc_sem.at[3])
    mask_load = pltpu.make_async_copy(mask_hbm, mask_v, loc_sem.at[4])
    who_load = pltpu.make_async_copy(who_hbm, who_v, loc_sem.at[5])
    for load in (f_load, who_load, mask_load, kv_load, wi_load, wo_load):
        load.start()

    barrier = pltpu.get_barrier_semaphore()
    peers = [at_t((me_t + j) % n_tp) for j in range(1, n_tp)]
    peers += [at_x(j) for j in range(1, nx)]
    peers += [at_z(d * w) for d in range(1, win + 1) for w in (1, -1)]
    peers += [
        ((z + d * w + nz) % nz * nx + (x + j) % nx, me_t)
        for d in range(1, far - win + 1) for w in (1, -1) for j in range(1, nx)
    ]
    for dev in peers:
        pl.semaphore_signal(barrier, inc=1, device_id=dev, device_id_type=MESH)

    onehot[...] = jnp.zeros_like(onehot)
    shape = (nz * n_blk, DH)
    slot_id = lax.broadcasted_iota(jnp.int32, shape, 0)
    lane = lax.broadcasted_iota(jnp.int32, shape, 1)
    ext = jnp.where(lane < users, FAR, 0.0)
    for u in range(users):
        hit = jnp.zeros(shape, jnp.bool_)
        for j in range(most):
            held = jnp.where(j < counts_ref[u], blocks_ref[u, j], -1)
            hit = jnp.logical_or(hit, slot_id == held)
        ext = jnp.where(jnp.logical_and(hit, lane == u), 0.0, ext)
    ext_v[...] = ext
    who_load.wait()
    who = who_v[...].astype(jnp.float32)

    def tables(ref, i, way, d):
        ref[i, 0 : who.shape[0]] = who
        for g in range(far - win + 1 if d == win else 1):
            holder = (z + (d + g) * (1 - 2 * way) + nz) % nz
            ref[i, 8 + 8 * g : 8 + 8 * g + n_blk] = ext_v[pl.ds(pl.multiple_of(holder * n_blk, n_blk), n_blk)]

    tables(info_all, 0, 0, 0)
    for way in range(2):
        for d in range(1, win + 1):
            tables(info_out, way * win + d, way, d)
    pl.semaphore_wait(barrier, len(peers))

    sends = []

    def go(copy):
        copy.start()
        sends.append(copy)

    partner = y * CORES + 1 - core

    def y_src(j, c):
        return (y - j + ny) % ny * CORES + c

    def y_sends(buf, c, ss, rs):
        own = buf.at[me_t, c]
        devs = [at_t(partner)] + [at_t((y + j) % ny * CORES + core) for j in range(1, ny)]
        return [rc(own, own, ss.at[c, j], rs.at[c, j], dev) for j, dev in enumerate(devs)]

    def y_passed(buf, c, ss, rs, j, side):
        got = buf.at[y_src(j, side), c]
        k = ny - 1 + j if j else 0
        return rc(got, got, ss.at[c, k], rs.at[c, k], at_t(partner))

    def y_forward(buf, c, ss, rs):
        for j in range(1, ny):
            got = buf.at[y_src(j, core), c]
            rc(got, got, ss.at[c, j], rs.at[c, j], at_t(partner)).wait_recv()
            y_passed(buf, c, ss, rs, j, core).start()

    def y_wait(buf, c, ss, rs):
        for j in range(ny):
            y_passed(buf, c, ss, rs, j, 1 - core).wait_recv()

    def y_drain(buf, c, ss, rs):
        for copy in y_sends(buf, c, ss, rs):
            copy.wait_send()
        for j in range(1, ny):
            y_passed(buf, c, ss, rs, j, core).wait_send()

    f_load.wait()
    for c in range(CHUNKS):
        for copy in y_sends(feats, c, f_ss, f_rs):
            copy.start()

    def info_copy(i, dev):
        return rc(info_out.at[i], info_all.at[i], info_ss.at[i], info_rs.at[i], dev)

    for way in range(2):
        for d in range(1, win + 1):
            go(info_copy(way * win + d, at_z(d * (1 - 2 * way))))

    def unit(way, d):
        return jnp.maximum(2 * d - 1 + way, 0) if not isinstance(d, int) else (2 * d - 1 + way if d else 0)

    def x_copy(u, j):
        return rc(snd.at[u, j], kvr.at[u, j], x_ss.at[u, j], x_rs.at[u, j], at_x(j))

    def hop_copy(way, d, j):
        u = unit(way, d)
        dev = ((z - (d - win) * (1 - 2 * way) + nz) % nz * nx + (x + j) % nx, me_t)
        if d < far:
            return rc(snd.at[u, j], kvr.at[u, j], x_ss.at[u, j], x_rs.at[u, j], dev)
        return rc(
            snd.at[2 * far - 1, j, way], kvr.at[u, j, way], x_ss.at[u, j], x_rs.at[u, j], dev
        )

    def prepare(n):
        way, d = (n + 1) % 2, far - (n + 1) // 2
        if isinstance(n, int) and d == far:
            way = 0
        u = unit(way, d)
        ranker = (z - d * (1 - 2 * way) + nz) % nz * nx

        def one(i, carry):
            j, c = i // CAP, i % CAP
            slot = slots_ref[c, ranker + (x + j) % nx]
            block = kv_v[slot]
            live = mask_v[slot].astype(jnp.float32).astype(jnp.bfloat16)
            snd[u, j, c, :, 0:DH] = block[:, 0:DH]
            snd[u, j, c, :, DH:] = block[:, DH:].T * live
            return carry

        lax.fori_loop(0, n_blk, one, 0)
        if isinstance(n, int) and d > win:
            for j in range(nx):
                for w in range(2) if d == far else (way,):
                    hop_copy(w, d, j).start()
        else:
            for j in range(1, nx):
                x_copy(u, j).start()

    def q_copy(way, d, c):
        before = 0 if d == 1 else way * win + d - 1
        return rc(
            qs.at[before, c], qs.at[way * win + d, c],
            q_ss.at[way, d, c], q_rs.at[way, d, c], at_z(1 - 2 * way),
        )

    def p_copy(way, d, c):
        return rc(
            parts.at[way, d - 1, c], incoming.at[way, d - 1, c],
            p_ss.at[way, d - 1, c], p_rs.at[way, d - 1, c], at_z(2 * way - 1),
        )

    def project(c):
        block = jnp.concatenate([feats[t, c] for t in range(n_tp)], axis=1)
        act = silu(jnp.dot(block, w_in_v[...], preferred_element_type=jnp.float32))
        qs[0, c] = act[:, 0:DH].T.astype(jnp.bfloat16)
        gates[c] = act[:, DH:].astype(jnp.bfloat16)

    def attend(i, c, blocks):
        user = lax.broadcasted_iota(jnp.int32, (16, DH), 0).astype(jnp.float32)
        per = rows // DH
        for r in range(per):
            row = info_all[i, pl.ds(c * per + r, 1), :]
            onehot[0:16, r * DH : (r + 1) * DH] = jnp.where(row == user, 1.0, 0.0).astype(jnp.bfloat16)
        keys, values = [], []
        for block, b in blocks:
            row = info_all[i, pl.ds(8 + b, 1), :].astype(jnp.bfloat16)
            keys.append(jnp.concatenate([block[:, 0:DH], jnp.broadcast_to(row, (EVENTS, DH))], axis=1))
            values.append(block[:, DH:])
        rhs = jnp.concatenate([qs[i, c], onehot[...]], axis=0)
        v = HALF_SCALE * jnp.dot(
            jnp.concatenate(keys, axis=0), rhs, preferred_element_type=jnp.float32
        )
        w = (v + v * jnp.tanh(v)).astype(jnp.bfloat16)
        return jnp.dot(jnp.concatenate(values, axis=1), w, preferred_element_type=jnp.float32)

    def entry(j, s):
        return (x - j + nx) % nx * CAP + s

    def near_blocks(u):
        return [
            (snd[u, 0, s] if j == 0 else kvr[u, j, s], entry(j, s)) for j in range(nx) for s in range(CAP)
        ]

    def edge_blocks(way):
        blocks = near_blocks(unit(way, win))
        for d in range(win + 1, far + 1):
            u = 2 * d - 1 + way
            for j in range(nx):
                if d < far:
                    blocks += [(kvr[u, j, s], 8 * (d - win) + entry(j, s)) for s in range(CAP)]
                else:
                    blocks += [(kvr[u, j, way], 8 * (d - win) + entry(j, way))]
        return blocks

    def in_range(c):
        return jnp.logical_and(c >= 0, c < CHUNKS)

    def tick(t, carry):
        @pl.when(t < CHUNKS)
        def _():
            y_wait(feats, t, f_ss, f_rs)
            project(t)
            for way in range(2):
                q_copy(way, 1, t).start()

        @pl.when(t + 1 < CHUNKS)
        def _():
            y_forward(feats, t + 1, f_ss, f_rs)

        for d in range(win - 1, 0, -1):
            c = t - d

            @pl.when(in_range(c))
            def _():
                for way in range(2):
                    q_copy(way, d, c).wait_recv()
                    q_copy(way, d + 1, c).start()

        @pl.when(t + 3 < nz)
        def _():
            prepare(t + 3)

        c = t - win

        @pl.when(in_range(c))
        def _():
            def edge(way, carry):
                i = way * win + win

                @pl.when(c == 0)
                def _():
                    for j in range(1, nx):
                        x_copy(unit(way, win), j).wait_recv()
                    for d in range(win + 1, far + 1):
                        for j in range(nx):
                            got = kvr.at[2 * d - 1 + way, j]
                            if d == far:
                                got = got.at[way]
                            sems = x_ss.at[2 * d - 1 + way, j], x_rs.at[2 * d - 1 + way, j]
                            rc(got, got, *sems, at_x(1)).wait_recv()
                    info_copy(i, at_z(1)).wait_recv()

                q_copy(way, win, c).wait_recv()
                parts[way, win - 1, c] = attend(i, c, edge_blocks(way)).astype(jnp.bfloat16)
                p_copy(way, win, c).start()
                return carry

            lax.fori_loop(0, 2, edge, 0)

        return carry

    def inner(m, carry):
        d, c, way = win - 1 - m // (2 * CHUNKS), m // 2 % CHUNKS, m % 2
        u, i = 2 * d - 1 + way, way * win + d

        @pl.when(c == 0)
        def _():
            for j in range(1, nx):
                x_copy(u, j).wait_recv()
            info_copy(i, at_z(1)).wait_recv()

        total = attend(i, c, near_blocks(u))
        p_copy(way, d + 1, c).wait_recv()
        got = incoming[way, d, c].astype(jnp.float32)
        parts[way, d - 1, c] = (total + got).astype(jnp.bfloat16)
        p_copy(way, d, c).start()
        return carry

    def finish(c, carry):
        total = attend(0, c, near_blocks(0))
        for way in range(2):
            p_copy(way, 1, c).wait_recv()
            total = total + incoming[way, 0, c].astype(jnp.float32)
        inv = lax.rsqrt(jnp.mean(total * total, axis=0, keepdims=True) + norm_eps)
        normed = (total * inv).T * gates[c].astype(jnp.float32)
        hid[me_t, c] = normed.astype(jnp.bfloat16)
        for copy in y_sends(hid, c, h_ss, h_rs):
            copy.start()
        return carry

    def output(t, carry):
        @pl.when(t < CHUNKS)
        def _():
            y_forward(hid, t, h_ss, h_rs)

        @pl.when(t > 0)
        def _():
            c = t - 1
            y_wait(hid, c, h_ss, h_rs)
            block = jnp.concatenate([hid[s, c] for s in range(n_tp)], axis=1)
            w_all = jnp.concatenate([w_out_all[s] for s in range(n_tp)], axis=0)
            mixed = jnp.dot(block, w_all, preferred_element_type=jnp.float32)
            out_ref[c] = (feats[me_t, c].astype(jnp.float32) + mixed).astype(jnp.bfloat16)

        return carry

    mask_load.wait()
    kv_load.wait()
    prepare(0)
    wi_load.wait()
    wo_load.wait()
    w_out_all[me_t] = w_out_v[:, pl.ds(pl.multiple_of(me_t * DH, DH), DH)]
    for j in range(1, n_tp):
        s = (me_t + j) % n_tp
        cols = pl.ds(pl.multiple_of(s * DH, DH), DH)
        go(rc(w_out_v.at[:, cols], w_out_all.at[me_t], w_ss.at[j], w_rs.at[j], at_t(s)))
    prepare(1)
    y_forward(feats, 0, f_ss, f_rs)
    prepare(2)
    lax.fori_loop(0, CHUNKS + win, tick, 0)
    lax.fori_loop(0, 2 * CHUNKS * (win - 1), inner, 0)
    for j in range(1, nx):
        x_copy(0, j).wait_recv()
    lax.fori_loop(0, CHUNKS, finish, 0)
    for j in range(1, n_tp):
        s = (me_t - j + n_tp) % n_tp
        rc(w_out_all.at[s], w_out_all.at[s], w_ss.at[j], w_rs.at[j], at_t(s)).wait_recv()
    lax.fori_loop(0, CHUNKS + 1, output, 0)

    for copy in sends:
        copy.wait_send()

    def drain(c, carry):
        y_drain(feats, c, f_ss, f_rs)
        y_drain(hid, c, h_ss, h_rs)
        for way in range(2):
            for d in range(1, win + 1):
                q_copy(way, d, c).wait_send()
                p_copy(way, d, c).wait_send()
        return carry

    lax.fori_loop(0, CHUNKS, drain, 0)
    for way in range(2):
        for d in range(win + 1, far + 1):
            for j in range(nx):
                hop_copy(way, d, j).wait_send()

    def drain_x(u, carry):
        for j in range(1, nx):
            x_copy(u, j).wait_send()
        return carry

    lax.fori_loop(0, 2 * win + 1, drain_x, 0)


def per_device(
    nz, cand_feats, w_in, w_out, kv_cache, event_mask, block_counts, user_blocks, send_slots, cand_user
):
    n_rows = cand_feats.shape[0]
    rows = n_rows // CHUNKS
    nx = lax.axis_size("user") // nz
    n_tp = lax.axis_size("tp")
    ny = n_tp // CORES
    far = nz // 2
    win = WINDOW
    units = 2 * far + 1
    tab = 8 * (far - win + 2)

    bf16, f32 = jnp.bfloat16, jnp.float32
    dma = pltpu.SemaphoreType.DMA
    hbm = pl.BlockSpec(memory_space=pltpu.HBM)
    smem = pl.BlockSpec(memory_space=pltpu.SMEM)
    mask = event_mask.reshape(-1, 1, EVENTS)
    who = cand_user.reshape(-1, DH)
    out = pl.pallas_call(
        functools.partial(kernel, (nz, nx, ny)),
        out_shape=jax.ShapeDtypeStruct((CHUNKS, rows, DH), bf16),
        in_specs=[smem] * 3 + [hbm] * 6,
        out_specs=pl.BlockSpec(memory_space=pltpu.VMEM),
        scratch_shapes=[
            pltpu.VMEM(who.shape, jnp.int32),
            pltpu.VMEM(mask.shape, jnp.int32),
            pltpu.VMEM(kv_cache.shape, bf16),
            pltpu.VMEM((units, nx, CAP, EVENTS, 2 * DH), bf16),
            pltpu.VMEM((units, nx, CAP, EVENTS, 2 * DH), bf16),
            pltpu.VMEM((n_tp, CHUNKS, rows, DH), bf16),
            pltpu.VMEM(w_in.shape, bf16),
            pltpu.VMEM(w_out.shape, bf16),
            pltpu.VMEM((n_tp, DH, DH), bf16),
            pltpu.VMEM((nz * nx * CAP, DH), f32),
            pltpu.VMEM((2 * win + 1, tab, DH), f32),
            pltpu.VMEM((2 * win + 1, tab, DH), f32),
            pltpu.VMEM((2 * win + 1, CHUNKS, DH, rows), bf16),
            pltpu.VMEM((CHUNKS, rows, DH), bf16),
            pltpu.VMEM((DH, rows), bf16),
            pltpu.VMEM((2, win, CHUNKS, DH, rows), bf16),
            pltpu.VMEM((2, win, CHUNKS, DH, rows), bf16),
            pltpu.VMEM((n_tp, CHUNKS, rows, DH), bf16),
            dma((6,)),
            dma((units, nx)),
            dma((units, nx)),
            dma((2 * win + 1,)),
            dma((2 * win + 1,)),
            dma((CHUNKS, 2 * ny - 1)),
            dma((CHUNKS, 2 * ny - 1)),
            dma((CHUNKS, 2 * ny - 1)),
            dma((CHUNKS, 2 * ny - 1)),
            dma((n_tp,)),
            dma((n_tp,)),
            dma((2, win + 1, CHUNKS)),
            dma((2, win + 1, CHUNKS)),
            dma((2, win, CHUNKS)),
            dma((2, win, CHUNKS)),
        ],
        compiler_params=pltpu.CompilerParams(
            collective_id=0, has_side_effects=True, vmem_limit_bytes=60 * 2**20
        ),
        name="score",
    )(
        send_slots.T,
        block_counts,
        user_blocks,
        who,
        mask,
        kv_cache,
        cand_feats.reshape(CHUNKS, rows, DH),
        w_in,
        w_out,
    )
    return out.reshape(n_rows, DH)


def solution(mesh):
    in_specs = (
        P("user", "tp"),
        P(None, "tp"),
        P("tp", None),
        P("user", None, "tp"),
        P("user", None),
        P("user"),
        P("user", None),
        P("user", None),
        P("user"),
    )
    return jax.shard_map(
        functools.partial(per_device, Z_SIZE),
        mesh=mesh,
        in_specs=in_specs,
        out_specs=P("user", "tp"),
        check_vma=False,
    )
```

time: 249 us -> 81 us (0.33)
  waiting for transfers between devices: 126 us -> 0 us
  Pallas kernels: 0 us -> 79.2 us
  matrix products: 43 us -> 0 us
  local copies, waits for them, and re-layouts: 44.6 us -> 1.67 us
  starting transfers between devices: 17.9 us -> 0 us
  between operations: 13.6 us -> 0.01 us
    pallas_call x0 -> x1, Pallas kernels: none -> 79.2 us  [per_device(): pl.pallas_call(functools.partial(kernel, (nz, nx, ny)), out_shape=jax.Sha...]
    all_to_all x2 -> x0, waiting for transfers between devices: 56.2 us -> none  [the longest x1 52.7 us: per_device(): lax.all_to_all(outgoing, 'user', split_axis=0, concat_axis=0, tiled=True)]
    dot_general x4 -> x0, matrix products: 43 us -> none  [the longest x2 38.9 us: one_block(): jnp.einsum('hre,ehd->rhd', attn_weights, value_rows, preferred_element_ty...]
    unnamed x3 -> x0, waiting for transfers between devices: 35.2 us -> none
    all_gather x1 -> x0, waiting for transfers between devices: 34.1 us -> none  [per_device(): lax.all_gather(cand_feats, 'tp', axis=1, tiled=True)]
    all_to_all x2 -> x0, starting transfers between devices: 17.8 us -> none  [the longest x1 11.9 us: per_device(): lax.all_to_all(out_marks, 'user', split_axis=0, concat_axis=0, tiled=True)]
    mul x2 -> x0, local copies, waits for them, and re-layouts: 14 us -> none  [one_block(): same_user[:, :, None] * live_mask[None]]
    slice x2 -> x0, local copies, waits for them, and re-layouts: 8.91 us -> none  [the longest x1 8.89 us: attend(): value_rows = pair_rows[:, :, 1, :]]
  transfers between devices with their start and end apart: 4 -> 0, of which waited for: 4 -> 0; matrix products, arithmetic and copies ran while one was open for 3% -> 0% of each run, Pallas kernels for 0% -> 0%
where the time goes in v2:
time: 81 us; the launch traced here: 80.9 us
  Pallas kernels  79.2 us (98%)
  local copies, waits for them, and re-layouts  1.67 us (2%)
    pallas_call x1, Pallas kernels, per_device(): pl.pallas_call(functools.partial(kernel, (nz, nx, ny)), out_shape=jax.Sha...  79.2 us
    unnamed x1, local copies, waits for them, and re-layouts  1.67 us

profile of v2, /device:TPU:1, one launch (start us, length us, event | category | flops | bytes accessed | tf_op | source)
XLA Modules:
  0.0 80.9 jit_solution(7664477810773908847)
XLA Ops:
  0.0 79.2 %score.1 = bf16[4,256,128]{2,1,0:T(8,128)(2,1)} custom-call(s32[2,32]{1,0:T(2,128)} %bitcast.9, s32[8]{0:T(128)} %counts_ref.1, s32[8,8]{1,0:T(8,128)} %blocks_ref.1, s32[8,128]{1,0:T(8,128)} %bitcast.8, s32[64,1,128]{2,1,0:T(1,128)} %bitcast.7, bf16[64,128,256]{2,1,0:T(8,128)(2,1)} %kv_hbm.1, bf16[4,256,128]{2,1,0:T(8,128)(2,1)} %bitcast.6, ...), custom_call_target="tpu_custom_call" | custom-call | tf_op jit(solution)/shard_map/score/pallas_call | solution.py:463
  79.2 1.7 %copy.11 = bf16[1024,128]{1,0:T(8,128)(2,1)} copy(bf16[1024,128]{1,0:T(8,128)(2,1)} %bitcast.5) | data formatting | bytes 524288

commit v3 on v2

--- a/solution.py
+++ b/solution.py
@@ -83,11 +83,23 @@
     z, x = me_u // nx, me_u % nx
     y, core = me_t // CORES, me_t % CORES
 
+    z_to = {d: ((z + d + nz) % nz * nx + x, me_t) for d in range(-win, win + 1)}
+    x_to = [(z * nx + (x + j) % nx, me_t) for j in range(nx)]
+    zx_to = {
+        (d, j): ((z + d + nz) % nz * nx + (x + j) % nx, me_t)
+        for d in range(win - far, far - win + 1) if d for j in range(nx)
+    }
+    partner = y * CORES + 1 - core
+    y_to = [(me_u, partner)] + [(me_u, (y + j) % ny * CORES + core) for j in range(1, ny)]
+    y_own = [(y - j + ny) % ny * CORES + core for j in range(ny)]
+    y_other = [(y - j + ny) % ny * CORES + 1 - core for j in range(ny)]
+    entries = [(x - j + nx) % nx * CAP for j in range(nx)]
+
     def at_z(d):
-        return ((z + d + nz) % nz * nx + x, me_t)
+        return z_to[d]
 
     def at_x(j):
-        return (z * nx + (x + j) % nx, me_t)
+        return x_to[j]
 
     def at_t(t):
         return (me_u, t)
@@ -97,15 +109,6 @@
             src_ref=src, dst_ref=dst, send_sem=ss, recv_sem=rs,
             device_id=dev, device_id_type=MESH,
         )
-
-    f_load = pltpu.make_async_copy(feats_hbm, feats.at[me_t], loc_sem.at[0])
-    kv_load = pltpu.make_async_copy(kv_hbm, kv_v, loc_sem.at[1])
-    wi_load = pltpu.make_async_copy(w_in_hbm, w_in_v, loc_sem.at[2])
-    wo_load = pltpu.make_async_copy(w_out_hbm, w_out_v, loc_sem.at[3])
-    mask_load = pltpu.make_async_copy(mask_hbm, mask_v, loc_sem.at[4])
-    who_load = pltpu.make_async_copy(who_hbm, who_v, loc_sem.at[5])
-    for load in (f_load, who_load, mask_load, kv_load, wi_load, wo_load):
-        load.start()
 
     barrier = pltpu.get_barrier_semaphore()
     peers = [at_t((me_t + j) % n_tp) for j in range(1, n_tp)]
@@ -117,6 +120,19 @@
     ]
     for dev in peers:
         pl.semaphore_signal(barrier, inc=1, device_id=dev, device_id_type=MESH)
+
+    f_load = pltpu.make_async_copy(feats_hbm, feats.at[me_t], loc_sem.at[0])
+    kv_step = kv_v.shape[0] // 8
+    kv_loads = [
+        pltpu.make_async_copy(kv_hbm.at[pl.ds(i * kv_step, kv_step)], kv_v.at[pl.ds(i * kv_step, kv_step)], loc_sem.at[6 + i])
+        for i in range(8)
+    ]
+    wi_load = pltpu.make_async_copy(w_in_hbm, w_in_v, loc_sem.at[2])
+    wo_load = pltpu.make_async_copy(w_out_hbm, w_out_v, loc_sem.at[3])
+    mask_load = pltpu.make_async_copy(mask_hbm, mask_v, loc_sem.at[4])
+    who_load = pltpu.make_async_copy(who_hbm, who_v, loc_sem.at[5])
+    for load in [f_load, mask_load, *kv_loads, who_load, wi_load, wo_load]:
+        load.start()
 
     onehot[...] = jnp.zeros_like(onehot)
     shape = (nz * n_blk, DH)
@@ -151,41 +167,37 @@
         copy.start()
         sends.append(copy)
 
-    partner = y * CORES + 1 - core
-
-    def y_src(j, c):
-        return (y - j + ny) % ny * CORES + c
-
-    def y_sends(buf, c, ss, rs):
+    def y_sends(buf, c, ss, rs, src=None):
         own = buf.at[me_t, c]
-        devs = [at_t(partner)] + [at_t((y + j) % ny * CORES + core) for j in range(1, ny)]
-        return [rc(own, own, ss.at[c, j], rs.at[c, j], dev) for j, dev in enumerate(devs)]
-
-    def y_passed(buf, c, ss, rs, j, side):
-        got = buf.at[y_src(j, side), c]
+        src = own if src is None else src
+        devs = y_to
+        return [rc(src, own, ss.at[c, j], rs.at[c, j], dev) for j, dev in enumerate(devs)]
+
+    def y_passed(buf, c, ss, rs, j, srcs):
+        got = buf.at[srcs[j], c]
         k = ny - 1 + j if j else 0
         return rc(got, got, ss.at[c, k], rs.at[c, k], at_t(partner))
 
     def y_forward(buf, c, ss, rs):
         for j in range(1, ny):
-            got = buf.at[y_src(j, core), c]
+            got = buf.at[y_own[j], c]
             rc(got, got, ss.at[c, j], rs.at[c, j], at_t(partner)).wait_recv()
-            y_passed(buf, c, ss, rs, j, core).start()
+            y_passed(buf, c, ss, rs, j, y_own).start()
 
     def y_wait(buf, c, ss, rs):
         for j in range(ny):
-            y_passed(buf, c, ss, rs, j, 1 - core).wait_recv()
+            y_passed(buf, c, ss, rs, j, y_other).wait_recv()
 
     def y_drain(buf, c, ss, rs):
         for copy in y_sends(buf, c, ss, rs):
             copy.wait_send()
         for j in range(1, ny):
-            y_passed(buf, c, ss, rs, j, core).wait_send()
-
+            y_passed(buf, c, ss, rs, j, y_own).wait_send()
+
+    for c in range(CHUNKS):
+        for copy in y_sends(feats, c, f_ss, f_rs, feats_hbm.at[c]):
+            copy.start()
     f_load.wait()
-    for c in range(CHUNKS):
-        for copy in y_sends(feats, c, f_ss, f_rs):
-            copy.start()
 
     def info_copy(i, dev):
         return rc(info_out.at[i], info_all.at[i], info_ss.at[i], info_rs.at[i], dev)
@@ -202,7 +214,7 @@
 
     def hop_copy(way, d, j):
         u = unit(way, d)
-        dev = ((z - (d - win) * (1 - 2 * way) + nz) % nz * nx + (x + j) % nx, me_t)
+        dev = zx_to[(win - d) * (1 - 2 * way), j]
         if d < far:
             return rc(snd.at[u, j], kvr.at[u, j], x_ss.at[u, j], x_rs.at[u, j], dev)
         return rc(
@@ -225,7 +237,7 @@
             snd[u, j, c, :, DH:] = block[:, DH:].T * live
             return carry
 
-        lax.fori_loop(0, n_blk, one, 0)
+        lax.fori_loop(0, n_blk, one, 0, unroll=4)
         if isinstance(n, int) and d > win:
             for j in range(nx):
                 for w in range(2) if d == far else (way,):
@@ -238,13 +250,18 @@
         before = 0 if d == 1 else way * win + d - 1
         return rc(
             qs.at[before, c], qs.at[way * win + d, c],
-            q_ss.at[way, d, c], q_rs.at[way, d, c], at_z(1 - 2 * way),
+            q_ss.at[way, d, c], q_rs.at[way, d, c], z_to[1 - 2 * way if isinstance(way, int) else 1],
         )
+
+    def inward(way):
+        if isinstance(way, int):
+            return z_to[2 * way - 1]
+        return (jnp.where(way == 0, z_to[-1][0], z_to[1][0]), me_t)
 
     def p_copy(way, d, c):
         return rc(
             parts.at[way, d - 1, c], incoming.at[way, d - 1, c],
-            p_ss.at[way, d - 1, c], p_rs.at[way, d - 1, c], at_z(2 * way - 1),
+            p_ss.at[way, d - 1, c], p_rs.at[way, d - 1, c], inward(way),
         )
 
     def project(c):
@@ -272,7 +289,7 @@
         return jnp.dot(jnp.concatenate(values, axis=1), w, preferred_element_type=jnp.float32)
 
     def entry(j, s):
-        return (x - j + nx) % nx * CAP + s
+        return entries[j] + s
 
     def near_blocks(u):
         return [
@@ -313,10 +330,6 @@
                 for way in range(2):
                     q_copy(way, d, c).wait_recv()
                     q_copy(way, d + 1, c).start()
-
-        @pl.when(t + 3 < nz)
-        def _():
-            prepare(t + 3)
 
         c = t - win
 
@@ -348,7 +361,7 @@
         return carry
 
     def inner(m, carry):
-        d, c, way = win - 1 - m // (2 * CHUNKS), m // 2 % CHUNKS, m % 2
+        d, c, way = win - 1 - m // (2 * CHUNKS), (m >> 1) & (CHUNKS - 1), m & 1
         u, i = 2 * d - 1 + way, way * win + d
 
         @pl.when(c == 0)
@@ -380,6 +393,11 @@
         @pl.when(t < CHUNKS)
         def _():
             y_forward(hid, t, h_ss, h_rs)
+            for copy in y_sends(hid, t, h_ss, h_rs):
+                copy.wait_send()
+            for way in range(2):
+                for d in range(1, win + 1):
+                    p_copy(way, d, t).wait_send()
 
         @pl.when(t > 0)
         def _():
@@ -389,12 +407,19 @@
             w_all = jnp.concatenate([w_out_all[s] for s in range(n_tp)], axis=0)
             mixed = jnp.dot(block, w_all, preferred_element_type=jnp.float32)
             out_ref[c] = (feats[me_t, c].astype(jnp.float32) + mixed).astype(jnp.bfloat16)
+            for j in range(1, ny):
+                y_passed(hid, c, h_ss, h_rs, j, y_own).wait_send()
 
         return carry
 
     mask_load.wait()
-    kv_load.wait()
+    for load in kv_loads:
+        load.wait()
     prepare(0)
+    prepare(1)
+    prepare(2)
+    lax.fori_loop(3, 8, lambda n, carry: (prepare(n), carry)[1], 0)
+    y_forward(feats, 0, f_ss, f_rs)
     wi_load.wait()
     wo_load.wait()
     w_out_all[me_t] = w_out_v[:, pl.ds(pl.multiple_of(me_t * DH, DH), DH)]
@@ -402,32 +427,19 @@
         s = (me_t + j) % n_tp
         cols = pl.ds(pl.multiple_of(s * DH, DH), DH)
         go(rc(w_out_v.at[:, cols], w_out_all.at[me_t], w_ss.at[j], w_rs.at[j], at_t(s)))
-    prepare(1)
-    y_forward(feats, 0, f_ss, f_rs)
-    prepare(2)
     lax.fori_loop(0, CHUNKS + win, tick, 0)
     lax.fori_loop(0, 2 * CHUNKS * (win - 1), inner, 0)
-    for j in range(1, nx):
-        x_copy(0, j).wait_recv()
-    lax.fori_loop(0, CHUNKS, finish, 0)
-    for j in range(1, n_tp):
-        s = (me_t - j + n_tp) % n_tp
-        rc(w_out_all.at[s], w_out_all.at[s], w_ss.at[j], w_rs.at[j], at_t(s)).wait_recv()
-    lax.fori_loop(0, CHUNKS + 1, output, 0)
-
     for copy in sends:
         copy.wait_send()
 
-    def drain(c, carry):
+    def drain_early(c, carry):
         y_drain(feats, c, f_ss, f_rs)
-        y_drain(hid, c, h_ss, h_rs)
         for way in range(2):
             for d in range(1, win + 1):
                 q_copy(way, d, c).wait_send()
-                p_copy(way, d, c).wait_send()
         return carry
 
-    lax.fori_loop(0, CHUNKS, drain, 0)
+    lax.fori_loop(0, CHUNKS, drain_early, 0)
     for way in range(2):
         for d in range(win + 1, far + 1):
             for j in range(nx):
@@ -438,7 +450,16 @@
             x_copy(u, j).wait_send()
         return carry
 
-    lax.fori_loop(0, 2 * win + 1, drain_x, 0)
+    lax.fori_loop(1, 2 * win + 1, drain_x, 0)
+    for j in range(1, n_tp):
+        s = (me_t - j + n_tp) % n_tp
+        rc(w_out_all.at[s], w_out_all.at[s], w_ss.at[j], w_rs.at[j], at_t(s)).wait_recv()
+    for j in range(1, nx):
+        x_copy(0, j).wait_recv()
+    lax.fori_loop(0, CHUNKS, finish, 0)
+    for j in range(1, nx):
+        x_copy(0, j).wait_send()
+    lax.fori_loop(0, CHUNKS + 1, output, 0)
 
 
 def per_device(
@@ -462,7 +483,7 @@
     who = cand_user.reshape(-1, DH)
     out = pl.pallas_call(
         functools.partial(kernel, (nz, nx, ny)),
-        out_shape=jax.ShapeDtypeStruct((CHUNKS, rows, DH), bf16),
+        out_shape=pltpu.VMEM((CHUNKS, rows, DH), bf16),
         in_specs=[smem] * 3 + [hbm] * 6,
         out_specs=pl.BlockSpec(memory_space=pltpu.VMEM),
         scratch_shapes=[
@@ -484,7 +505,7 @@
             pltpu.VMEM((2, win, CHUNKS, DH, rows), bf16),
             pltpu.VMEM((2, win, CHUNKS, DH, rows), bf16),
             pltpu.VMEM((n_tp, CHUNKS, rows, DH), bf16),
-            dma((6,)),
+            dma((14,)),
             dma((units, nx)),
             dma((units, nx)),
             dma((2 * win + 1,)),

time: 81 us -> 78.2 us (0.965)
  Pallas kernels: 79.2 us -> 77.4 us
  local copies, waits for them, and re-layouts: 1.67 us -> 0.71 us
    pallas_call x1, Pallas kernels: 79.2 us -> 77.4 us  [per_device(): pl.pallas_call(functools.partial(kernel, (nz, nx, ny)), out_shape=pltpu.V...]
    unnamed x1, local copies, waits for them, and re-layouts: 1.67 us -> 0.71 us
where the time goes in v3:
time: 78.2 us; the launch traced here: 78.1 us
  Pallas kernels  77.4 us (99%)
    pallas_call x1, Pallas kernels, per_device(): pl.pallas_call(functools.partial(kernel, (nz, nx, ny)), out_shape=pltpu.V...  77.4 us

profile of v3, /device:TPU:1, one launch (start us, length us, event | category | flops | bytes accessed | tf_op | source)
XLA Modules:
  0.0 78.1 jit_solution(16780329830449668047)
XLA Ops:
  0.0 77.4 %score.1 = bf16[4,256,128]{2,1,0:T(8,128)(2,1)S(1)} custom-call(s32[2,32]{1,0:T(2,128)} %bitcast.9, s32[8]{0:T(128)} %counts_ref.1, s32[8,8]{1,0:T(8,128)} %blocks_ref.1, s32[8,128]{1,0:T(8,128)} %bitcast.8, s32[64,1,128]{2,1,0:T(1,128)} %bitcast.7, bf16[64,128,256]{2,1,0:T(8,128)(2,1)} %kv_hbm.1, bf16[4,256,128]{2,1,0:T(8,128)(2,1)} %bitcast.6, ...), custom_call_target="tpu_custom_call" | custom-call | tf_op jit(solution)/shard_map/score/pallas_call | solution.py:484
  77.4 0.7 copy.11

commit v4 on v3

--- a/solution.py
+++ b/solution.py
@@ -171,7 +171,7 @@
         own = buf.at[me_t, c]
         src = own if src is None else src
         devs = y_to
-        return [rc(src, own, ss.at[c, j], rs.at[c, j], dev) for j, dev in enumerate(devs)]
+        return [rc(src, own, ss.at[c, j], rs.at[c, j], devs[j]) for j in (2, 1, 3, 0)]
 
     def y_passed(buf, c, ss, rs, j, srcs):
         got = buf.at[srcs[j], c]
@@ -237,7 +237,7 @@
             snd[u, j, c, :, DH:] = block[:, DH:].T * live
             return carry
 
-        lax.fori_loop(0, n_blk, one, 0, unroll=4)
+        lax.fori_loop(0, n_blk, one, 0, unroll=8)
         if isinstance(n, int) and d > win:
             for j in range(nx):
                 for w in range(2) if d == far else (way,):

time: 78.2 us -> 77.9 us (level)
  no operation moved by 1% of the time
where the time goes in v4:
time: 77.9 us; the launch traced here: 77.8 us
  Pallas kernels  77.1 us (99%)
    pallas_call x1, Pallas kernels, per_device(): pl.pallas_call(functools.partial(kernel, (nz, nx, ny)), out_shape=pltpu.V...  77.1 us

profile of v4, /device:TPU:1, one launch (start us, length us, event | category | flops | bytes accessed | tf_op | source)
XLA Modules:
  0.0 77.8 jit_solution(11439225763655904721)
XLA Ops:
  0.0 77.1 %score.1 = bf16[4,256,128]{2,1,0:T(8,128)(2,1)S(1)} custom-call(s32[2,32]{1,0:T(2,128)} %bitcast.9, s32[8]{0:T(128)} %counts_ref.1, s32[8,8]{1,0:T(8,128)} %blocks_ref.1, s32[8,128]{1,0:T(8,128)} %bitcast.8, s32[64,1,128]{2,1,0:T(1,128)} %bitcast.7, bf16[64,128,256]{2,1,0:T(8,128)(2,1)} %kv_hbm.1, bf16[4,256,128]{2,1,0:T(8,128)(2,1)} %bitcast.6, ...), custom_call_target="tpu_custom_call" | custom-call | tf_op jit(solution)/shard_map/score/pallas_call | solution.py:484
  77.1 0.7 copy.11
